TPU v7x, 512 devices: a whole 4x4x16 slice. The times are simulated.
512 devices in a mesh: tens: 8 (over y, core), atom: 64 (over z, x).
Axes of the slice: x: 4, y: 4, z: 16, core: 2. Of those that a mesh axis runs over, the one named last changes fastest.
Arguments:
- chibar: float32 [384, 16384], P(None, 'atom'), may hold values from -6 to 6
- t_blocks: float32 [384, 786432], P(None, ('tens', 'atom')), may hold values from -0.3125 to 0.3125
- n_saved: float32 [384, 786432], P('tens', 'atom'), may hold values from -0.0390625 to 0.0390625
- q_list: int32 [8, 64, 3], P('tens', 'atom'), may hold values from 0 to 13, as said below
- q_count: int32 [8, 64], P('tens', 'atom'), may hold values from 1 to 3, as said below
Outputs:
- gbar: float32 [4096, 320], P('atom')
Inputs may be any that keep to these rules, and one draw needn't show every extreme that they name: `q_list`: the 3 entries of one pair owner's list name blocks of 3 distinct atom indices. `q_count`: equal to 3 on at least one pair owner.
All inputs are finite; a program needn't handle non-finite values.
Results may differ from a plain program's by a relative error of at most 0.0003.
Values sent between devices are 32-bit elements; how exact they have to be, the bound alone decides.
A program may use at most 64 MiB of HBM per device.

v0:
```python
import jax
import jax.numpy as jnp
from jax import lax
from jax.sharding import PartitionSpec as P

BLK = 128
ORB_DEV = 64
QB_DEV = 2
REACH = 3
QL = 3


def shifted(x, axis, by):
    devices = lax.axis_size(axis)
    return lax.ppermute(x, axis, [(i, (i + by) % devices) for i in range(devices)])


def place_block(block, offset, orb_width):
    return jnp.pad(block, ((0, 0), (offset * orb_width, (2 - offset) * orb_width)))


def assemble(blocks):
    moved = []
    for by_step, row_block in ((1, 2), (-1, 0)):
        moved.append(shifted(blocks[row_block], "atom", by_step))
    return (
        place_block(moved[0], 0, ORB_DEV)
        + place_block(blocks[1], 1, ORB_DEV)
        + place_block(moved[1], 2, ORB_DEV)
    )


def local(chibar, t_blocks, n_saved, q_list, q_count):
    highest = lax.Precision.HIGHEST
    p_window = chibar.shape[0]
    band_width = 3 * ORB_DEV
    slot_ids = q_list.reshape(QL)
    in_use = q_count.reshape(())
    keeper = (jnp.arange(QL) < in_use).astype(jnp.float32)
    pieces = []
    for offset in range(-REACH, REACH + 1):
        if offset == 0:
            pieces.append(chibar)
        else:
            pieces.append(shifted(chibar, "atom", -offset))
    neighbour = jnp.concatenate(pieces, axis=1).reshape(p_window, (2 * REACH + 1) * QB_DEV, BLK)
    chosen = jnp.take(neighbour, slot_ids, axis=1)
    chosen = (chosen * keeper[None, :, None]).reshape(p_window, QL * BLK)
    mbar_local = jnp.dot(chosen, t_blocks, precision=highest, preferred_element_type=jnp.float32)
    regrouped = lax.all_to_all(mbar_local, "tens", split_axis=0, concat_axis=1, tiled=True)
    p_rows = regrouped.shape[0]
    partial_value = jnp.einsum(
        "pnm,pml->nl",
        regrouped.reshape(p_rows, band_width, ORB_DEV),
        n_saved.reshape(p_rows, ORB_DEV, band_width),
        precision=highest,
    )
    result = lax.psum(assemble(partial_value.reshape(3, ORB_DEV, band_width)), "tens")
    return result


def solution(mesh):
    placed = (
        P(None, "atom"),
        P(None, ("tens", "atom")),
        P("tens", "atom"),
        P("tens", "atom", None),
        P("tens", "atom"),
    )
    return jax.shard_map(
        local, mesh=mesh, in_specs=placed, out_specs=P("atom", None), check_vma=False
    )
```

profile of v0, /device:TPU:1, one launch (start us, length us, event | category | flops | bytes accessed | tf_op | source)
XLA Modules:
  0.0 229.3 jit_solution(1775159750431050628)
XLA Ops:
  6.5 1.3 copy.6
  7.9 12.9 %collective-permute-start.5 = (f32[384,256]{0,1:T(8,128)S(1)}, f32[384,256]{0,1:T(8,128)S(1)}, u32[]{:S(2)}, u32[]{:S(2)}) collective-permute-start(f32[384,256]{0,1:T(8,128)S(1)} %copy.6), channel_id=1, source_target_pairs={{0,61},{1,62},{2,63},{3,0},{4,1},{5,2},{6,3},{7,4},{8,5},{9,6},{10... | collective-permute-start | bytes 1179656 | tf_op jit(solution)/shard_map/ppermute | solution.py:15
  20.7 4.8 %collective-permute-start.4 = (f32[384,256]{0,1:T(8,128)S(1)}, f32[384,256]{0,1:T(8,128)S(1)}, u32[]{:S(2)}, u32[]{:S(2)}) collective-permute-start(f32[384,256]{0,1:T(8,128)S(1)} %copy.6), channel_id=1, source_target_pairs={{0,62},{1,63},{2,0},{3,1},{4,2},{5,3},{6,4},{7,5},{8,6},{9,7},{10,... | collective-permute-start | bytes 1179656 | tf_op jit(solution)/shard_map/ppermute | solution.py:15
  25.5 1.9 collective-permute-start.2
  27.5 3.8 %collective-permute-start.1 = (f32[384,256]{0,1:T(8,128)S(1)}, f32[384,256]{0,1:T(8,128)S(1)}, u32[]{:S(2)}, u32[]{:S(2)}) collective-permute-start(f32[384,256]{0,1:T(8,128)S(1)} %copy.6), channel_id=1, source_target_pairs={{0,2},{1,3},{2,4},{3,5},{4,6},{5,7},{6,8},{7,9},{8,10},{9,11},{10,... | collective-permute-start | bytes 1179656 | tf_op jit(solution)/shard_map/ppermute | solution.py:15
  31.3 3.2 %collective-permute-start = (f32[384,256]{0,1:T(8,128)S(1)}, f32[384,256]{0,1:T(8,128)S(1)}, u32[]{:S(2)}, u32[]{:S(2)}) collective-permute-start(f32[384,256]{0,1:T(8,128)S(1)} %copy.6), channel_id=1, source_target_pairs={{0,3},{1,4},{2,5},{3,6},{4,7},{5,8},{6,9},{7,10},{8,11},{9,12},{10... | collective-permute-start | bytes 1179656 | tf_op jit(solution)/shard_map/ppermute | solution.py:15
  36.6 8.8 %collective-permute-done = f32[384,256]{0,1:T(8,128)S(1)} collective-permute-done((f32[384,256]{0,1:T(8,128)S(1)}, f32[384,256]{0,1:T(8,128)S(1)}, u32[]{:S(2)}, u32[]{:S(2)}) %collective-permute-start) | collective-permute-done | bytes 393248 | tf_op jit(solution)/shard_map/ppermute | solution.py:15
  45.4 20.1 %collective-permute-start.3 = (f32[384,256]{0,1:T(8,128)S(1)}, f32[384,256]{0,1:T(8,128)S(1)}, u32[]{:S(2)}, u32[]{:S(2)}) collective-permute-start(f32[384,256]{0,1:T(8,128)S(1)} %copy.6), channel_id=1, source_target_pairs={{0,63},{1,0},{2,1},{3,2},{4,3},{5,4},{6,5},{7,6},{8,7},{9,8},{10,9... | collective-permute-start | bytes 1179656 | tf_op jit(solution)/shard_map/ppermute | solution.py:15
  65.5 0.8 constant_dynamic-update-slice_fusion.6
  66.3 0.8 constant_dynamic-update-slice_fusion.5
  67.0 0.8 constant_dynamic-update-slice_fusion.4
  67.8 0.8 constant_dynamic-update-slice_fusion.3
  68.6 3.1 %collective-permute-done.3 = f32[384,256]{0,1:T(8,128)S(1)} collective-permute-done((f32[384,256]{0,1:T(8,128)S(1)}, f32[384,256]{0,1:T(8,128)S(1)}, u32[]{:S(2)}, u32[]{:S(2)}) %collective-permute-start.3) | collective-permute-done | bytes 393248 | tf_op jit(solution)/shard_map/ppermute | solution.py:15
  71.7 0.8 constant_dynamic-update-slice_fusion.2
  72.5 0.8 constant_dynamic-update-slice_fusion.1
  73.3 0.8 constant_dynamic-update-slice_fusion
  74.0 3.4 %copy.13 = f32[384,14,128]{2,0,1:T(8,128)} copy(f32[384,14,128]{0,2,1:T(8,128)} %bitcast.2) | data formatting | bytes 5505024 | tf_op jit(solution)/shard_map/reshape | solution.py:46
  77.4 2.4 %gather_fusion = f32[3,384,128]{2,1,0:T(8,128)S(1)} fusion(f32[384,14,128]{2,0,1:T(8,128)} %copy.13, s32[1024]{0:T(1024)S(1)} %pad_clamp_fusion), kind=kCustom, calls=%fused_computation | custom fusion | bytes 1179660 | tf_op jit(solution)/shard_map/jit(_take)/gather | solution.py:47
  79.8 1.3 copy.14
  81.0 1.5 gather.7
  82.6 5.3 %fusion = f32[8,48,1536]{2,1,0:T(8,128)} fusion(f32[384,1536]{1,0:T(8,128)S(1)} %copy-done, f32[8,48,384]{2,1,0:T(8,128)S(1)} %gather.7, f32[384]{0:T(512)S(1)} %broadcast_bitcast_fusion, pred[384]{0:T(512)(128)(4,1)S(1)} %broadcast_bitcast_fusion.1), kind=kOutput, calls=%fused_computation.1 | convolution fusion | flops 2718203904 | bytes 5310336 | tf_op jit(solution)/shard_map/dot_general | solution.py:49
  87.8 7.5 %all-to-all-start = ((f32[8,48,1536]{2,1,0:T(8,128)}), f32[8,48,1536]{2,1,0:T(8,128)}, u32[]{:S(2)}, u32[]{:S(2)}) async-start(f32[8,48,1536]{2,1,0:T(8,128)} %fusion), calls=%async_computation | async-start | bytes 4718592 | tf_op jit(solution)/shard_map/all_to_all | solution.py:50
  95.4 3.9 %reshape.88 = f32[48,64,192]{2,1,0:T(8,128)} reshape(f32[48,12288]{1,0:T(8,128)} %param.7) | data formatting | bytes 4718592 | tf_op jit(solution)/shard_map/reshape | solution.py:55
  99.3 25.4 %all-to-all-done = f32[8,48,1536]{2,1,0:T(8,128)} async-done(((f32[8,48,1536]{2,1,0:T(8,128)}), f32[8,48,1536]{2,1,0:T(8,128)}, u32[]{:S(2)}, u32[]{:S(2)}) %all-to-all-start) | async-done | bytes 2359328 | tf_op jit(solution)/shard_map/all_to_all | solution.py:50
  124.6 4.5 %copy.15 = f32[48,8,1536]{2,1,0:T(8,128)} copy(f32[48,8,1536]{2,0,1:T(8,128)} %bitcast.9) | data formatting | bytes 4718592 | tf_op jit(solution)/shard_map/all_to_all | solution.py:50
  129.2 4.7 %reshape.87 = f32[48,192,64]{2,1,0:T(8,128)} reshape(f32[48,8,1536]{2,1,0:T(8,128)} %copy.15) | data formatting | bytes 4718592 | tf_op jit(solution)/shard_map/reshape | solution.py:54
  133.8 7.4 %convolution_bitcast_fusion = f32[192,192]{1,0:T(8,128)S(1)} fusion(f32[48,192,64]{2,1,0:T(8,128)} %reshape.87, f32[48,64,192]{2,1,0:T(8,128)} %reshape.88), kind=kOutput, calls=%fused_computation.3 | convolution fusion | flops 1358954496 | bytes 4866048 | tf_op jit(solution)/shard_map/pnm,pml->nl/dot_general | solution.py:52
  141.2 4.3 %collective-permute-start.6 = (f32[64,192]{1,0:T(8,128)S(1)}, f32[64,192]{1,0:T(8,128)S(1)}, u32[]{:S(2)}, u32[]{:S(2)}) collective-permute-start(f32[64,192]{1,0:T(8,128)S(1)} %get-tuple-element.5), channel_id=1, source_target_pairs={{0,1},{1,2},{2,3},{3,4},{4,5},{5,6},{6,7},{7,8},{8,9},{9,10},{10,1... | collective-permute-start | bytes 147464 | tf_op jit(solution)/shard_map/ppermute | solution.py:15
  145.5 5.1 %collective-permute-start.7 = (f32[64,192]{1,0:T(8,128)S(1)}, f32[64,192]{1,0:T(8,128)S(1)}, u32[]{:S(2)}, u32[]{:S(2)}) collective-permute-start(f32[64,192]{1,0:T(8,128)S(1)} %get-tuple-element.6), channel_id=1, source_target_pairs={{0,63},{1,0},{2,1},{3,2},{4,3},{5,4},{6,5},{7,6},{8,7},{9,8},{10,9... | collective-permute-start | bytes 147464 | tf_op jit(solution)/shard_map/ppermute | solution.py:15
  150.6 1.3 collective-permute-done.7
  152.7 68.2 %all-reduce.5.cloned.1.call-done = f32[64,320]{1,0:T(8,128)} async-done(((f32[64,320]{1,0:T(8,128)}), f32[64,320]{1,0:T(8,128)}) %all-reduce.5.cloned.1.call-update) | async-done | bytes 81936 | tf_op jit(solution)/shard_map/psum | solution.py:58
  220.9 1.5 copy.26
  (17 shorter events, 2.3 us)
Async XLA Ops:
  6.5 76.0 %copy-start = (f32[384,1536]{1,0:T(8,128)S(1)}, f32[384,1536]{1,0:T(8,128)}, u32[]{:S(2)}) copy-start(f32[384,1536]{1,0:T(8,128)} %param.6) | copy-start | bytes 7077892
  7.9 65.4 %collective-permute-start.5 = (f32[384,256]{0,1:T(8,128)S(1)}, f32[384,256]{0,1:T(8,128)S(1)}, u32[]{:S(2)}, u32[]{:S(2)}) collective-permute-start(f32[384,256]{0,1:T(8,128)S(1)} %copy.6), channel_id=1, source_target_pairs={{0,61},{1,62},{2,63},{3,0},{4,1},{5,2},{6,3},{7,4},{8,5},{9,6},{10... | collective-permute-start | bytes 1179656 | tf_op jit(solution)/shard_map/ppermute | solution.py:15
  20.7 51.7 %collective-permute-start.4 = (f32[384,256]{0,1:T(8,128)S(1)}, f32[384,256]{0,1:T(8,128)S(1)}, u32[]{:S(2)}, u32[]{:S(2)}) collective-permute-start(f32[384,256]{0,1:T(8,128)S(1)} %copy.6), channel_id=1, source_target_pairs={{0,62},{1,63},{2,0},{3,1},{4,2},{5,3},{6,4},{7,5},{8,6},{9,7},{10,... | collective-permute-start | bytes 1179656 | tf_op jit(solution)/shard_map/ppermute | solution.py:15
  25.5 41.5 %collective-permute-start.2 = (f32[384,256]{0,1:T(8,128)S(1)}, f32[384,256]{0,1:T(8,128)S(1)}, u32[]{:S(2)}, u32[]{:S(2)}) collective-permute-start(f32[384,256]{0,1:T(8,128)S(1)} %copy.6), channel_id=1, source_target_pairs={{0,1},{1,2},{2,3},{3,4},{4,5},{5,6},{6,7},{7,8},{8,9},{9,10},{10,1... | collective-permute-start | bytes 1179656 | tf_op jit(solution)/shard_map/ppermute | solution.py:15
  27.5 38.8 %collective-permute-start.1 = (f32[384,256]{0,1:T(8,128)S(1)}, f32[384,256]{0,1:T(8,128)S(1)}, u32[]{:S(2)}, u32[]{:S(2)}) collective-permute-start(f32[384,256]{0,1:T(8,128)S(1)} %copy.6), channel_id=1, source_target_pairs={{0,2},{1,3},{2,4},{3,5},{4,6},{5,7},{6,8},{7,9},{8,10},{9,11},{10,... | collective-permute-start | bytes 1179656 | tf_op jit(solution)/shard_map/ppermute | solution.py:15
  31.3 14.1 %collective-permute-start = (f32[384,256]{0,1:T(8,128)S(1)}, f32[384,256]{0,1:T(8,128)S(1)}, u32[]{:S(2)}, u32[]{:S(2)}) collective-permute-start(f32[384,256]{0,1:T(8,128)S(1)} %copy.6), channel_id=1, source_target_pairs={{0,3},{1,4},{2,5},{3,6},{4,7},{5,8},{6,9},{7,10},{8,11},{9,12},{10... | collective-permute-start | bytes 1179656 | tf_op jit(solution)/shard_map/ppermute | solution.py:15
  45.4 26.4 %collective-permute-start.3 = (f32[384,256]{0,1:T(8,128)S(1)}, f32[384,256]{0,1:T(8,128)S(1)}, u32[]{:S(2)}, u32[]{:S(2)}) collective-permute-start(f32[384,256]{0,1:T(8,128)S(1)} %copy.6), channel_id=1, source_target_pairs={{0,63},{1,0},{2,1},{3,2},{4,3},{5,4},{6,5},{7,6},{8,7},{9,8},{10,9... | collective-permute-start | bytes 1179656 | tf_op jit(solution)/shard_map/ppermute | solution.py:15
  87.8 36.8 %all-to-all-start = ((f32[8,48,1536]{2,1,0:T(8,128)}), f32[8,48,1536]{2,1,0:T(8,128)}, u32[]{:S(2)}, u32[]{:S(2)}) async-start(f32[8,48,1536]{2,1,0:T(8,128)} %fusion), calls=%async_computation | async-start | bytes 4718592 | tf_op jit(solution)/shard_map/all_to_all | solution.py:50
  95.4 125.5 %all-reduce.5.cloned.1.call-start = ((), (), s32[]{:S(2)}) async-start(), calls=%async_computation.1 | async-start | bytes 196608 | tf_op jit(solution)/shard_map/psum | solution.py:58
  141.2 9.4 %collective-permute-start.6 = (f32[64,192]{1,0:T(8,128)S(1)}, f32[64,192]{1,0:T(8,128)S(1)}, u32[]{:S(2)}, u32[]{:S(2)}) collective-permute-start(f32[64,192]{1,0:T(8,128)S(1)} %get-tuple-element.5), channel_id=1, source_target_pairs={{0,1},{1,2},{2,3},{3,4},{4,5},{5,6},{6,7},{7,8},{8,9},{9,10},{10,1... | collective-permute-start | bytes 147464 | tf_op jit(solution)/shard_map/ppermute | solution.py:15
  145.5 6.4 %collective-permute-start.7 = (f32[64,192]{1,0:T(8,128)S(1)}, f32[64,192]{1,0:T(8,128)S(1)}, u32[]{:S(2)}, u32[]{:S(2)}) collective-permute-start(f32[64,192]{1,0:T(8,128)S(1)} %get-tuple-element.6), channel_id=1, source_target_pairs={{0,63},{1,0},{2,1},{3,2},{4,3},{5,4},{6,5},{7,6},{8,7},{9,8},{10,9... | collective-permute-start | bytes 147464 | tf_op jit(solution)/shard_map/ppermute | solution.py:15
Sparse Core Ops, SparseCore 0:
  152.8 68.0 all-reduce.4
where the time goes:
time: 230 us; the launch traced here: 229 us
  waiting for transfers between devices  107 us (47%)
  starting transfers between devices  63.6 us (28%)
  local copies, waits for them, and re-layouts  29.9 us (13%)
  between operations  14.2 us (6%)
  matrix products  12.7 us (6%)
    psum x1, waiting for transfers between devices, local(): lax.psum(assemble(partial_value.reshape(3, ORB_DEV, band_width)), 'tens')  68.2 us
    ppermute x8, starting transfers between devices, shifted(): lax.ppermute(x, axis, [(i, (i + by) % devices) for i in range(devices)])  56 us
    all_to_all x1, waiting for transfers between devices, local(): lax.all_to_all(mbar_local, 'tens', split_axis=0, concat_axis=1, tiled=True)  25.4 us
    ppermute x8, waiting for transfers between devices, shifted(): lax.ppermute(x, axis, [(i, (i + by) % devices) for i in range(devices)])  13.2 us
    all_to_all x1, starting transfers between devices, local(): lax.all_to_all(mbar_local, 'tens', split_axis=0, concat_axis=1, tiled=True)  7.55 us
    unnamed x10, local copies, waits for them, and re-layouts  7.48 us
    dot_general x1, matrix products, local(): jnp.einsum('pnm,pml->nl', regrouped.reshape(p_rows, band_width, ORB_DEV),...  7.4 us
    dot_general x1, matrix products, local(): jnp.dot(chosen, t_blocks, precision=highest, preferred_element_type=jnp.f...  5.29 us
  transfers between devices with their start and end apart: 10, of which 5 were waited for; matrix products, arithmetic and copies ran while one was open for 4% of the time, Pallas kernels for 0%

commit v1 on v0

v1 whole, which is shorter than its diff:
```python
import jax
import jax.numpy as jnp
from jax import lax
from jax.experimental import pallas as pl
from jax.experimental.pallas import tpu as pltpu
from jax.sharding import PartitionSpec as P

F32 = jnp.float32
BF16 = jnp.bfloat16
MESH = pl.DeviceIdType.MESH
REACH = 3
STAGES = 4
SHIFTS = (1, -1, 2, -2, 3, -3)


def split(x):
    high = x.astype(BF16)
    return high, (x - high.astype(F32)).astype(BF16)


def dot(a, b):
    return jnp.dot(a, b, preferred_element_type=F32)


def dot3(a_high, a_low, b_high, b_low):
    return dot(a_high, b_high) + (dot(a_high, b_low) + dot(a_low, b_high))


def kernel(n_tens, n_atom, chibar, t_blocks, n_saved, q_list_in, q_count_in, out, q_list, q_count,
           t_full, t_high, t_low, n_full, n_left, n_right, n_high, n_low,
           near0, near1, near2, near3, past0, past1, past2, past3, mbar_out, mbar_in, part_out, part_in, home_in, total, final,
           q_sem, t_sem, n_sem, own_sem, chi_send, chi_recv, fwd_send, fwd_recv,
           mbar_send, mbar_recv, part_send, part_recv, home_send, home_recv, fin_send, fin_recv):
    near = (near0, near1, near2, near3)
    past = (past0, past1, past2, past3)
    t = lax.axis_index("tens")
    s = lax.axis_index("atom")
    y = t // 2
    c = lax.rem(t, 2)
    chips = n_tens // 2

    def device(chip, core):
        return lax.rem(chip + chips, chips) * 2 + core

    def atom(by):
        return lax.rem(s + by + n_atom, n_atom)

    chip_to = (y + 2, y + 1 - 2 * c, y - 1 + 2 * c, y)
    chip_to2 = (y + 2, y - 1 + 2 * c, y + 1 - 2 * c, y)
    chip_from = (y + 2, y - 1 + 2 * c, y + 1 - 2 * c, y)

    def target(k, e):
        return device(chip_to[k], c) if e == 0 else device(chip_to2[k], 1 - c)

    def source(k, e):
        return device(chip_from[k], c if e == 0 else 1 - c)

    sibling = device(y, 1 - c)

    load_q = (pltpu.make_async_copy(q_list_in, q_list, q_sem.at[0]), pltpu.make_async_copy(q_count_in, q_count, q_sem.at[1]))
    for copy in load_q:
        copy.start()
    load_t = pltpu.make_async_copy(t_blocks, t_full, t_sem)
    load_n = pltpu.make_async_copy(n_saved, n_full, n_sem)
    load_t.start()
    own = []
    for k in range(STAGES):
        rows = pl.ds(pl.multiple_of(target(k, 0) * 48, 48), 48)
        own.append(pltpu.make_async_copy(chibar.at[rows], near[k].at[REACH], own_sem.at[k]))
        own[k].start()
    load_n.start()

    barrier = pltpu.get_barrier_semaphore()
    for by in SHIFTS:
        pl.semaphore_signal(barrier, inc=1, device_id=(t, atom(by)), device_id_type=MESH)
    for by in range(1, n_tens):
        pl.semaphore_signal(barrier, inc=1, device_id=(lax.rem(t + by, n_tens), s), device_id_type=MESH)
    pl.semaphore_wait(barrier, len(SHIFTS) + n_tens - 1)

    chi = []
    for k in range(STAGES):
        rows = pl.ds(pl.multiple_of(target(k, 0) * 48, 48), 48)
        chi.append([
            pltpu.make_async_remote_copy(
                src_ref=chibar.at[rows],
                dst_ref=near[k].at[REACH - by],
                send_sem=chi_send.at[k, i],
                recv_sem=chi_recv.at[k, i],
                device_id=(t, atom(by)),
                device_id_type=MESH,
            )
            for i, by in enumerate(SHIFTS)
        ])
    for copy in chi[0]:
        copy.start()

    load_t.wait()

    def split_t(i, _):
        rows = pl.ds(pl.multiple_of(i * 16, 16), 16)
        t_high[rows], t_low[rows] = split(t_full[rows])
        return _

    lax.fori_loop(0, 24, split_t, 0)
    low_half = lax.broadcasted_iota(jnp.int32, (8, 128), 1) < 64

    def lay_n(m, _):
        base = pl.multiple_of(m * 384, 384)
        for p in range(6):
            rows = pl.ds(p * 8, 8)
            first = n_full[rows, pl.ds(base, 128)]
            second = n_full[rows, pl.ds(base + 128, 128)]
            third = n_full[rows, pl.ds(base + 256, 128)]
            second_r = pltpu.roll(second, 64, 1)
            third_r = pltpu.roll(third, 64, 1)
            start = (p % 3) * 8 * 128 + (p // 3) * 64 + 2 * m
            n_left[pl.ds(start, 8, stride=128), :] = first
            n_right[pl.ds(start, 8, stride=128), :] = second
            n_left[pl.ds(start + 1, 8, stride=128), :] = jnp.where(low_half, second_r, third_r)
            n_right[pl.ds(start + 1, 8, stride=128), :] = third_r
        return _

    def split_n(i, _):
        rows = pl.ds(pl.multiple_of(i * 64, 64), 64)
        n_high[rows, 0:128], n_low[rows, 0:128] = split(n_left[rows])
        n_high[rows, 128:256], n_low[rows, 128:256] = split(n_right[rows])
        return _


    mbar = []
    for k in range(STAGES):
        mbar.append([
            pltpu.make_async_remote_copy(
                src_ref=mbar_out.at[2 * k + e],
                dst_ref=mbar_in.at[2 * k + e],
                send_sem=mbar_send.at[2 * k + e],
                recv_sem=mbar_recv.at[2 * k + e],
                device_id=(target(k, e), s),
                device_id_type=MESH,
            )
            for e in range(2)
        ])

    forward = [
        pltpu.make_async_remote_copy(
            src_ref=near[k],
            dst_ref=past[k],
            send_sem=fwd_send.at[k],
            recv_sem=fwd_recv.at[k],
            device_id=(sibling, s),
            device_id_type=MESH,
        )
        for k in range(STAGES)
    ]
    half_of = lax.broadcasted_iota(jnp.int32, (24, 128), 1) < 64

    def compute(k, e):
        pieces = []
        for q in range(3):
            name = q_list[0, 0, q]
            block = (past if e else near)[k][name // 2]
            piece = jnp.where(lax.rem(name, 2) == 0, block[:, :128], block[:, 128:])
            pieces.append(jnp.where(q < q_count[0, 0], piece, jnp.zeros_like(piece)))
        high, low = split(jnp.concatenate(pieces, axis=1))
        for j in range(6):
            cols = pl.ds(j * 256, 256)
            r = dot3(high, low, t_high[:, cols], t_low[:, cols])
            for i in range(2):
                r0 = r[:24, i * 128:(i + 1) * 128]
                r1 = r[24:, i * 128:(i + 1) * 128]
                even = jnp.where(half_of, r0, pltpu.roll(r1, 64, 1))
                odd = jnp.where(half_of, pltpu.roll(r0, 64, 1), r1)
                nu = j * 4 + i * 2
                for g in range(3):
                    mbar_out[2 * k + e, pl.ds(g * 192 + nu, 8, stride=24), :] = even[g * 8:(g + 1) * 8]
                    mbar_out[2 * k + e, pl.ds(g * 192 + nu + 1, 8, stride=24), :] = odd[g * 8:(g + 1) * 8]

    for copy in load_q:
        copy.wait()
    for k in range(STAGES):
        own[k].wait()
        for copy in chi[k]:
            copy.wait_recv()
        forward[k].start()
        if k < 3:
            for copy in chi[k + 1]:
                copy.start()
        compute(k, 0)
        if k < 3:
            mbar[k][0].start()
        forward[k].wait_recv()
        compute(k, 1)
        mbar[k][1].start()
        if k == 0:
            load_n.wait()
            lax.fori_loop(0, 32, lay_n, 0)
        if k == 1:
            lax.fori_loop(0, 48, split_n, 0)

    def side(o):
        return jnp.where(o < 3, -1, jnp.where(o > 4, 1, 0))

    def straddles(o):
        return jnp.logical_or(o == 2, o == 5)

    def part(i, o):
        return pltpu.make_async_remote_copy(
            src_ref=part_out.at[i], dst_ref=part_in.at[i], send_sem=part_send.at[i], recv_sem=part_recv.at[i],
            device_id=(o, atom(side(o))), device_id_type=MESH)

    def part_home(i, o):
        return pltpu.make_async_remote_copy(
            src_ref=part_out.at[i], dst_ref=home_in.at[i], send_sem=home_send.at[i], recv_sem=home_recv.at[i],
            device_id=(o, s), device_id_type=MESH)

    inner = side(t) == 0
    edge = straddles(t)

    for k in (0, 3, 1, 2):
        if k < 3:
            mbar[k][0].wait_recv()
        mbar[k][1].wait_recv()
        first = mbar_out if k == 3 else mbar_in
        acc = jnp.zeros((48, 256), F32)
        for g in range(6):
            highs, lows = [], []
            for p in range(4):
                rows = pl.ds((g * 4 + p) * 24, 24)
                high, low = split(jnp.concatenate([first[2 * k, rows, :], mbar_in[2 * k + 1, rows, :]], axis=0))
                highs.append(high)
                lows.append(low)
            rows = pl.ds(g * 512, 512)
            acc = acc + dot3(jnp.concatenate(highs, axis=1), jnp.concatenate(lows, axis=1), n_high[rows], n_low[rows])
        part_out[2 * k] = acc[:24]
        part_out[2 * k + 1] = acc[24:]
        for e in range(2):
            i, o = 2 * k + e, source(k, e)
            if i == 6:
                @pl.when(jnp.logical_not(inner))
                def _():
                    part(6, t).start()
            else:
                part(i, o).start()

                @pl.when(straddles(o))
                def _():
                    part_home(i, o).start()

    order = (0, 1, 7, 2, 3, 4, 5)

    @pl.when(inner)
    def _():
        part_in[6] = part_out[6]

    @pl.when(jnp.logical_not(inner))
    def _():
        part(6, t).wait_recv()

    summed = part_in[6]
    for i in order:
        part(i, source(i // 2, i % 2)).wait_recv()
        summed = summed + part_in[i]
    total[...] = summed

    @pl.when(edge)
    def _():
        near_sum = part_out[6]
        for i in order:
            part_home(i, source(i // 2, i % 2)).wait_recv()
            near_sum = near_sum + home_in[i]
        row = lax.broadcasted_iota(jnp.int32, (24, 256), 0)
        least = jnp.where(t == 2, 16, 0)
        from_home = jnp.logical_and(row >= least, row < least + 8)
        total[...] = jnp.where(from_home, near_sum, total[...])

    def share(i):
        return pltpu.make_async_remote_copy(
            src_ref=total, dst_ref=final.at[t], send_sem=fin_send.at[i], recv_sem=fin_recv.at[n_tens - i],
            device_id=(lax.rem(t + i, n_tens), s), device_id_type=MESH)

    for i in (4, 3, 5, 2, 6, 1, 7):
        share(i).start()
    final[t] = total[...]
    for i in range(1, n_tens):
        share(i).wait_recv()

    lower = jnp.concatenate([final[5, 8:24, :], final[6], final[7]], axis=0)
    mid = jnp.concatenate([final[2, 16:24, :], final[3], final[4], final[5, 0:8, :]], axis=0)
    upper = jnp.concatenate([final[0], final[1], final[2, 0:16, :]], axis=0)
    half = lax.broadcasted_iota(jnp.int32, (64, 128), 1) < 64
    mid0 = pltpu.roll(mid[:, :128], 64, 1)
    mid1 = pltpu.roll(mid[:, 128:], 64, 1)
    zero = jnp.zeros((64, 128), F32)
    out[:, 0:128] = lower[:, :128] + jnp.where(half, zero, mid0)
    out[:, 128:256] = jnp.where(half, lower[:, 128:], zero) + jnp.where(half, mid0, mid1) + upper[:, :128]
    out[:, 256:320] = upper[:, 128:192]

    for k in range(STAGES):
        for copy in chi[k]:
            copy.wait_send()
        forward[k].wait_send()
        for e in range(2):
            if (k, e) != (3, 0):
                mbar[k][e].wait_send()
    for i in order:
        o = source(i // 2, i % 2)
        part(i, o).wait_send()

        @pl.when(straddles(o))
        def _():
            part_home(i, o).wait_send()

    @pl.when(jnp.logical_not(inner))
    def _():
        part(6, t).wait_send()

    for i in range(1, n_tens):
        share(i).wait_send()


def local(n_tens, n_atom, chibar, t_blocks, n_saved, q_list, q_count):
    def body(*refs):
        kernel(n_tens, n_atom, *refs)

    hbm = pl.BlockSpec(memory_space=pltpu.HBM)
    dma = pltpu.SemaphoreType.DMA
    return pl.pallas_call(
        body,
        out_shape=jax.ShapeDtypeStruct((64, 320), F32),
        in_specs=[hbm] * 5,
        out_specs=pl.BlockSpec(memory_space=pltpu.VMEM),
        scratch_shapes=[
            pltpu.SMEM((1, 1, 3), jnp.int32),
            pltpu.SMEM((1, 1), jnp.int32),
            pltpu.VMEM((384, 1536), F32),
            pltpu.VMEM((384, 1536), BF16),
            pltpu.VMEM((384, 1536), BF16),
            pltpu.VMEM((48, 12288), F32),
            pltpu.VMEM((3072, 128), F32),
            pltpu.VMEM((3072, 128), F32),
            pltpu.VMEM((3072, 256), BF16),
            pltpu.VMEM((3072, 256), BF16),
        ]
        + [pltpu.VMEM((7, 48, 256), F32)] * (2 * STAGES)
        + [
            pltpu.VMEM((8, 576, 128), F32),
            pltpu.VMEM((8, 576, 128), F32),
            pltpu.VMEM((8, 24, 256), F32),
            pltpu.VMEM((8, 24, 256), F32),
            pltpu.VMEM((8, 24, 256), F32),
            pltpu.VMEM((24, 256), F32),
            pltpu.VMEM((8, 24, 256), F32),
            dma((2,)), dma, dma, dma((STAGES,)), dma((STAGES, 6)), dma((STAGES, 6)), dma((STAGES,)), dma((STAGES,)),
            dma((8,)), dma((8,)), dma((8,)), dma((8,)), dma((8,)), dma((8,)), dma((8,)), dma((8,)),
        ],
        compiler_params=pltpu.CompilerParams(
            collective_id=0, has_side_effects=True, vmem_limit_bytes=63 * 2**20
        ),
        name="gradient",
    )(chibar, t_blocks, n_saved, q_list, q_count)


def solution(mesh):
    sizes = mesh.shape
    placed = (
        P(None, "atom"),
        P(None, ("tens", "atom")),
        P("tens", "atom"),
        P("tens", "atom", None),
        P("tens", "atom"),
    )

    def step(*args):
        return local(sizes["tens"], sizes["atom"], *args)

    return jax.shard_map(step, mesh=mesh, in_specs=placed, out_specs=P("atom", None), check_vma=False)
```

time: 230 us -> 63.7 us (0.28)
  waiting for transfers between devices: 107 us -> 0 us
  starting transfers between devices: 63.6 us -> 0 us
  Pallas kernels: 0 us -> 61.3 us
  local copies, waits for them, and re-layouts: 29.9 us -> 1.54 us
  between operations: 14.2 us -> 0.66 us
  matrix products: 12.7 us -> 0 us
    psum x1 -> x0, waiting for transfers between devices: 68.2 us -> none  [local(): lax.psum(assemble(partial_value.reshape(3, ORB_DEV, band_width)), 'tens')]
    pallas_call x0 -> x1, Pallas kernels: none -> 61.3 us  [local(): pl.pallas_call(body, out_shape=jax.ShapeDtypeStruct((64, 320), F32), in_s...]
    ppermute x8 -> x0, starting transfers between devices: 56 us -> none  [shifted(): lax.ppermute(x, axis, [(i, (i + by) % devices) for i in range(devices)])]
    all_to_all x1 -> x0, waiting for transfers between devices: 25.4 us -> none  [local(): lax.all_to_all(mbar_local, 'tens', split_axis=0, concat_axis=1, tiled=True)]
    ppermute x8 -> x0, waiting for transfers between devices: 13.2 us -> none  [shifted(): lax.ppermute(x, axis, [(i, (i + by) % devices) for i in range(devices)])]
    dot_general x2 -> x0, matrix products: 12.7 us -> none  [the longest x1 7.4 us: local(): jnp.einsum('pnm,pml->nl', regrouped.reshape(p_rows, band_width, ORB_DEV),...]
    reshape x3 -> x0, local copies, waits for them, and re-layouts: 11.9 us -> none  [the longest x1 4.65 us: local(): regrouped.reshape(p_rows, band_width, ORB_DEV)]
    all_to_all x1 -> x0, starting transfers between devices: 7.55 us -> none  [local(): lax.all_to_all(mbar_local, 'tens', split_axis=0, concat_axis=1, tiled=True)]
  transfers between devices with their start and end apart: 10 -> 0, of which waited for: 5 -> 0; matrix products, arithmetic and copies ran while one was open for 4% -> 0% of each run, Pallas kernels for 0% -> 0%
where the time goes in v1:
time: 63.7 us; the launch traced here: 63.5 us
  Pallas kernels  61.3 us (96%)
  local copies, waits for them, and re-layouts  1.54 us (2%)
  between operations  0.66 us (1%)
    pallas_call x1, Pallas kernels, local(): pl.pallas_call(body, out_shape=jax.ShapeDtypeStruct((64, 320), F32), in_s...  61.3 us
    unnamed x1, local copies, waits for them, and re-layouts  1.54 us

profile of v1, /device:TPU:1, one launch (start us, length us, event | category | flops | bytes accessed | tf_op | source)
XLA Modules:
  0.0 63.5 jit_solution(18109760045405580623)
XLA Ops:
  0.7 61.3 %gradient.1 = f32[64,320]{1,0:T(8,128)} custom-call(f32[384,256]{1,0:T(8,128)} %refs_0_.1, f32[384,1536]{1,0:T(8,128)} %refs_1_.1, f32[48,12288]{1,0:T(8,128)} %refs_2_.1, s32[1,1,3]{2,1,0:T(1,128)} %refs_3_.1, s32[1,1]{1,0:T(1,128)S(6)} %copy.7.refs_4_), custom_call_target="tpu_custom_call" | custom-call | tf_op jit(solution)/shard_map/gradient/pallas_call | solution.py:327
  62.0 1.5 %copy.8 = f32[64,320]{1,0:T(8,128)} copy(f32[64,320]{1,0:T(8,128)} %gradient.1) | data formatting | bytes 163840

commit v2 on v1

--- a/solution.py
+++ b/solution.py
@@ -10,6 +10,7 @@
 MESH = pl.DeviceIdType.MESH
 REACH = 3
 STAGES = 4
+STEPS = ((0, 0, 16), (0, 16, 32), (1, 0, 48), (2, 0, 48), (3, 0, 48))
 SHIFTS = (1, -1, 2, -2, 3, -3)
 
 
@@ -23,16 +24,18 @@
 
 
 def dot3(a_high, a_low, b_high, b_low):
-    return dot(a_high, b_high) + (dot(a_high, b_low) + dot(a_low, b_high))
+    rows = a_high.shape[0]
+    both = dot(jnp.concatenate([a_high, a_low], axis=0), b_high)
+    return both[:rows] + (both[rows:] + dot(a_high, b_low))
 
 
 def kernel(n_tens, n_atom, chibar, t_blocks, n_saved, q_list_in, q_count_in, out, q_list, q_count,
            t_full, t_high, t_low, n_full, n_left, n_right, n_high, n_low,
-           near0, near1, near2, near3, past0, past1, past2, past3, mbar_out, mbar_in, part_out, part_in, home_in, total, final,
+           near0, near1, near2, near3, near4, past0, past1, past2, past3, past4, mbar_out, mbar_in, part_out, part_in, home_in, total, final,
            q_sem, t_sem, n_sem, own_sem, chi_send, chi_recv, fwd_send, fwd_recv,
            mbar_send, mbar_recv, part_send, part_recv, home_send, home_recv, fin_send, fin_recv):
-    near = (near0, near1, near2, near3)
-    past = (past0, past1, past2, past3)
+    near = (near0, near1, near2, near3, near4)
+    past = (past0, past1, past2, past3, past4)
     t = lax.axis_index("tens")
     s = lax.axis_index("atom")
     y = t // 2
@@ -58,51 +61,34 @@
     sibling = device(y, 1 - c)
 
     load_q = (pltpu.make_async_copy(q_list_in, q_list, q_sem.at[0]), pltpu.make_async_copy(q_count_in, q_count, q_sem.at[1]))
+    load_t = pltpu.make_async_copy(t_blocks, t_full, t_sem)
+    load_n = pltpu.make_async_copy(n_saved, n_full, n_sem)
+    own = []
+
+    def rows_of(step):
+        k, first, rows = STEPS[step]
+        return pl.ds(pl.multiple_of(target(k, 0) * 48 + first, 16), rows)
+
+    for i in range(len(STEPS)):
+        own.append(pltpu.make_async_copy(chibar.at[rows_of(i)], near[i].at[REACH], own_sem.at[i]))
+        own[i].start()
+    load_t.start()
+    load_n.start()
     for copy in load_q:
         copy.start()
-    load_t = pltpu.make_async_copy(t_blocks, t_full, t_sem)
-    load_n = pltpu.make_async_copy(n_saved, n_full, n_sem)
-    load_t.start()
-    own = []
-    for k in range(STAGES):
-        rows = pl.ds(pl.multiple_of(target(k, 0) * 48, 48), 48)
-        own.append(pltpu.make_async_copy(chibar.at[rows], near[k].at[REACH], own_sem.at[k]))
-        own[k].start()
-    load_n.start()
-
-    barrier = pltpu.get_barrier_semaphore()
-    for by in SHIFTS:
-        pl.semaphore_signal(barrier, inc=1, device_id=(t, atom(by)), device_id_type=MESH)
-    for by in range(1, n_tens):
-        pl.semaphore_signal(barrier, inc=1, device_id=(lax.rem(t + by, n_tens), s), device_id_type=MESH)
-    pl.semaphore_wait(barrier, len(SHIFTS) + n_tens - 1)
-
-    chi = []
-    for k in range(STAGES):
-        rows = pl.ds(pl.multiple_of(target(k, 0) * 48, 48), 48)
-        chi.append([
-            pltpu.make_async_remote_copy(
-                src_ref=chibar.at[rows],
-                dst_ref=near[k].at[REACH - by],
-                send_sem=chi_send.at[k, i],
-                recv_sem=chi_recv.at[k, i],
-                device_id=(t, atom(by)),
-                device_id_type=MESH,
-            )
-            for i, by in enumerate(SHIFTS)
-        ])
-    for copy in chi[0]:
-        copy.start()
-
-    load_t.wait()
-
-    def split_t(i, _):
-        rows = pl.ds(pl.multiple_of(i * 16, 16), 16)
-        t_high[rows], t_low[rows] = split(t_full[rows])
-        return _
-
-    lax.fori_loop(0, 24, split_t, 0)
+
     low_half = lax.broadcasted_iota(jnp.int32, (8, 128), 1) < 64
+
+    def prepare():
+        load_t.wait()
+
+        def split_t(i, _):
+            rows = pl.ds(pl.multiple_of(i * 16, 16), 16)
+            t_high[rows], t_low[rows] = split(t_full[rows])
+            return _
+
+        lax.fori_loop(0, 24, split_t, 0)
+
 
     def lay_n(m, _):
         base = pl.multiple_of(m * 384, 384)
@@ -113,89 +99,95 @@
             third = n_full[rows, pl.ds(base + 256, 128)]
             second_r = pltpu.roll(second, 64, 1)
             third_r = pltpu.roll(third, 64, 1)
-            start = (p % 3) * 8 * 128 + (p // 3) * 64 + 2 * m
+            start = (p // 2) * 8 * 128 + (p % 2) * 64 + 2 * m
             n_left[pl.ds(start, 8, stride=128), :] = first
             n_right[pl.ds(start, 8, stride=128), :] = second
             n_left[pl.ds(start + 1, 8, stride=128), :] = jnp.where(low_half, second_r, third_r)
             n_right[pl.ds(start + 1, 8, stride=128), :] = third_r
         return _
 
+
     def split_n(i, _):
         rows = pl.ds(pl.multiple_of(i * 64, 64), 64)
         n_high[rows, 0:128], n_low[rows, 0:128] = split(n_left[rows])
         n_high[rows, 128:256], n_low[rows, 128:256] = split(n_right[rows])
         return _
 
-
-    mbar = []
-    for k in range(STAGES):
-        mbar.append([
+    barrier = pltpu.get_barrier_semaphore()
+    for by in SHIFTS:
+        pl.semaphore_signal(barrier, inc=1, device_id=(t, atom(by)), device_id_type=MESH)
+    for by in range(1, n_tens):
+        pl.semaphore_signal(barrier, inc=1, device_id=(lax.rem(t + by, n_tens), s), device_id_type=MESH)
+    pl.semaphore_wait(barrier, len(SHIFTS) + n_tens - 1)
+
+    chi = [
+        [
             pltpu.make_async_remote_copy(
-                src_ref=mbar_out.at[2 * k + e],
-                dst_ref=mbar_in.at[2 * k + e],
-                send_sem=mbar_send.at[2 * k + e],
-                recv_sem=mbar_recv.at[2 * k + e],
-                device_id=(target(k, e), s),
+                src_ref=near[step].at[REACH],
+                dst_ref=near[step].at[REACH - by],
+                send_sem=chi_send.at[step, i],
+                recv_sem=chi_recv.at[step, i],
+                device_id=(t, atom(by)),
                 device_id_type=MESH,
             )
-            for e in range(2)
-        ])
+            for i, by in enumerate(SHIFTS)
+        ]
+        for step in range(len(STEPS))
+    ]
+    for copy in own:
+        copy.wait()
+    for step in (0, 1):
+        for copy in chi[step]:
+            copy.start()
+    prepare()
+
+    def mbar(step, e):
+        k, first, rows = STEPS[step]
+        part_rows = pl.ds(first * 12, rows * 12)
+        return pltpu.make_async_remote_copy(
+            src_ref=mbar_out.at[2 * k + e, part_rows],
+            dst_ref=mbar_in.at[2 * k + e, part_rows],
+            send_sem=mbar_send.at[2 * step + e],
+            recv_sem=mbar_recv.at[2 * step + e],
+            device_id=(target(k, e), s),
+            device_id_type=MESH,
+        )
 
     forward = [
         pltpu.make_async_remote_copy(
-            src_ref=near[k],
-            dst_ref=past[k],
-            send_sem=fwd_send.at[k],
-            recv_sem=fwd_recv.at[k],
+            src_ref=near[i],
+            dst_ref=past[i],
+            send_sem=fwd_send.at[i],
+            recv_sem=fwd_recv.at[i],
             device_id=(sibling, s),
             device_id_type=MESH,
         )
-        for k in range(STAGES)
+        for i in range(len(STEPS))
     ]
-    half_of = lax.broadcasted_iota(jnp.int32, (24, 128), 1) < 64
-
-    def compute(k, e):
+
+    def compute(step, e):
+        k, first, rows = STEPS[step]
         pieces = []
         for q in range(3):
             name = q_list[0, 0, q]
-            block = (past if e else near)[k][name // 2]
+            block = (past if e else near)[step][name // 2]
             piece = jnp.where(lax.rem(name, 2) == 0, block[:, :128], block[:, 128:])
             pieces.append(jnp.where(q < q_count[0, 0], piece, jnp.zeros_like(piece)))
         high, low = split(jnp.concatenate(pieces, axis=1))
         for j in range(6):
             cols = pl.ds(j * 256, 256)
             r = dot3(high, low, t_high[:, cols], t_low[:, cols])
-            for i in range(2):
-                r0 = r[:24, i * 128:(i + 1) * 128]
-                r1 = r[24:, i * 128:(i + 1) * 128]
-                even = jnp.where(half_of, r0, pltpu.roll(r1, 64, 1))
-                odd = jnp.where(half_of, pltpu.roll(r0, 64, 1), r1)
-                nu = j * 4 + i * 2
-                for g in range(3):
-                    mbar_out[2 * k + e, pl.ds(g * 192 + nu, 8, stride=24), :] = even[g * 8:(g + 1) * 8]
-                    mbar_out[2 * k + e, pl.ds(g * 192 + nu + 1, 8, stride=24), :] = odd[g * 8:(g + 1) * 8]
-
-    for copy in load_q:
-        copy.wait()
-    for k in range(STAGES):
-        own[k].wait()
-        for copy in chi[k]:
-            copy.wait_recv()
-        forward[k].start()
-        if k < 3:
-            for copy in chi[k + 1]:
-                copy.start()
-        compute(k, 0)
-        if k < 3:
-            mbar[k][0].start()
-        forward[k].wait_recv()
-        compute(k, 1)
-        mbar[k][1].start()
-        if k == 0:
-            load_n.wait()
-            lax.fori_loop(0, 32, lay_n, 0)
-        if k == 1:
-            lax.fori_loop(0, 48, split_n, 0)
+            for g in range(rows // 16):
+                for i in range(2):
+                    r0 = r[g * 16:g * 16 + 8, i * 128:(i + 1) * 128]
+                    r1 = r[g * 16 + 8:g * 16 + 16, i * 128:(i + 1) * 128]
+                    even = jnp.where(low_half, r0, pltpu.roll(r1, 64, 1))
+                    odd = jnp.where(low_half, pltpu.roll(r0, 64, 1), r1)
+                    at = first * 12 + g * 192 + j * 4 + i * 2
+                    mbar_out[2 * k + e, pl.ds(at, 8, stride=24), :] = even
+                    mbar_out[2 * k + e, pl.ds(at + 1, 8, stride=24), :] = odd
+
+    steps_of = ((0, 1), (2,), (3,), (4,))
 
     def side(o):
         return jnp.where(o < 3, -1, jnp.where(o > 4, 1, 0))
@@ -216,10 +208,11 @@
     inner = side(t) == 0
     edge = straddles(t)
 
-    for k in (0, 3, 1, 2):
-        if k < 3:
-            mbar[k][0].wait_recv()
-        mbar[k][1].wait_recv()
+    def contract(k):
+        for step in steps_of[k]:
+            if k < 3:
+                mbar(step, 0).wait_recv()
+            mbar(step, 1).wait_recv()
         first = mbar_out if k == 3 else mbar_in
         acc = jnp.zeros((48, 256), F32)
         for g in range(6):
@@ -246,6 +239,46 @@
                 def _():
                     part_home(i, o).start()
 
+    def settle():
+        for step in range(len(STEPS)):
+            for copy in chi[step]:
+                copy.wait_send()
+            forward[step].wait_send()
+
+    def fetch(step):
+        for copy in chi[step]:
+            copy.start()
+
+    for copy in load_q:
+        copy.wait()
+    for step in range(len(STEPS)):
+        for copy in chi[step]:
+            copy.wait_recv()
+        forward[step].start()
+        for later in ((2,), (3,), (4,), (), ())[step]:
+            fetch(later)
+        compute(step, 0)
+        if step < 4:
+            mbar(step, 0).start()
+        forward[step].wait_recv()
+        compute(step, 1)
+        mbar(step, 1).start()
+        if step == 0:
+            load_n.wait()
+        if step < 4:
+            lax.fori_loop(8 * step, 8 * step + 8, lay_n, 0)
+        else:
+            lax.fori_loop(0, 48, split_n, 0)
+
+    settle()
+    for k in (3, 0, 1, 2):
+        contract(k)
+
+    for step in range(len(STEPS)):
+        if step < 4:
+            mbar(step, 0).wait_send()
+        mbar(step, 1).wait_send()
+
     order = (0, 1, 7, 2, 3, 4, 5)
 
     @pl.when(inner)
@@ -281,6 +314,18 @@
     for i in (4, 3, 5, 2, 6, 1, 7):
         share(i).start()
     final[t] = total[...]
+    for i in order:
+        o = source(i // 2, i % 2)
+        part(i, o).wait_send()
+
+        @pl.when(straddles(o))
+        def _():
+            part_home(i, o).wait_send()
+
+    @pl.when(jnp.logical_not(inner))
+    def _():
+        part(6, t).wait_send()
+
     for i in range(1, n_tens):
         share(i).wait_recv()
 
@@ -294,25 +339,6 @@
     out[:, 0:128] = lower[:, :128] + jnp.where(half, zero, mid0)
     out[:, 128:256] = jnp.where(half, lower[:, 128:], zero) + jnp.where(half, mid0, mid1) + upper[:, :128]
     out[:, 256:320] = upper[:, 128:192]
-
-    for k in range(STAGES):
-        for copy in chi[k]:
-            copy.wait_send()
-        forward[k].wait_send()
-        for e in range(2):
-            if (k, e) != (3, 0):
-                mbar[k][e].wait_send()
-    for i in order:
-        o = source(i // 2, i % 2)
-        part(i, o).wait_send()
-
-        @pl.when(straddles(o))
-        def _():
-            part_home(i, o).wait_send()
-
-    @pl.when(jnp.logical_not(inner))
-    def _():
-        part(6, t).wait_send()
 
     for i in range(1, n_tens):
         share(i).wait_send()
@@ -341,7 +367,7 @@
             pltpu.VMEM((3072, 256), BF16),
             pltpu.VMEM((3072, 256), BF16),
         ]
-        + [pltpu.VMEM((7, 48, 256), F32)] * (2 * STAGES)
+        + [pltpu.VMEM((7, rows, 256), F32) for _, _, rows in STEPS] * 2
         + [
             pltpu.VMEM((8, 576, 128), F32),
             pltpu.VMEM((8, 576, 128), F32),
@@ -350,8 +376,8 @@
             pltpu.VMEM((8, 24, 256), F32),
             pltpu.VMEM((24, 256), F32),
             pltpu.VMEM((8, 24, 256), F32),
-            dma((2,)), dma, dma, dma((STAGES,)), dma((STAGES, 6)), dma((STAGES, 6)), dma((STAGES,)), dma((STAGES,)),
-            dma((8,)), dma((8,)), dma((8,)), dma((8,)), dma((8,)), dma((8,)), dma((8,)), dma((8,)),
+            dma((2,)), dma, dma, dma((5,)), dma((5, 6)), dma((5, 6)), dma((5,)), dma((5,)),
+            dma((10,)), dma((10,)), dma((8,)), dma((8,)), dma((8,)), dma((8,)), dma((8,)), dma((8,)),
         ],
         compiler_params=pltpu.CompilerParams(
             collective_id=0, has_side_effects=True, vmem_limit_bytes=63 * 2**20

time: 63.7 us -> 63.6 us (level)
  no operation moved by 1% of the time
where the time goes in v2:
time: 63.6 us; the launch traced here: 63.5 us
  Pallas kernels  61.3 us (96%)
  local copies, waits for them, and re-layouts  1.54 us (2%)
  between operations  0.66 us (1%)
    pallas_call x1, Pallas kernels, local(): pl.pallas_call(body, out_shape=jax.ShapeDtypeStruct((64, 320), F32), in_s...  61.3 us
    unnamed x1, local copies, waits for them, and re-layouts  1.54 us

profile of v2, /device:TPU:1, one launch (start us, length us, event | category | flops | bytes accessed | tf_op | source)
XLA Modules:
  0.0 63.5 jit_solution(818862130864618912)
XLA Ops:
  0.7 61.3 %gradient.1 = f32[64,320]{1,0:T(8,128)} custom-call(f32[384,256]{1,0:T(8,128)} %refs_0_.1, f32[384,1536]{1,0:T(8,128)} %refs_1_.1, f32[48,12288]{1,0:T(8,128)} %refs_2_.1, s32[1,1,3]{2,1,0:T(1,128)} %refs_3_.1, s32[1,1]{1,0:T(1,128)S(6)} %copy.7.refs_4_), custom_call_target="tpu_custom_call" | custom-call | tf_op jit(solution)/shard_map/gradient/pallas_call | solution.py:353
  62.0 1.5 %copy.8 = f32[64,320]{1,0:T(8,128)} copy(f32[64,320]{1,0:T(8,128)} %gradient.1) | data formatting | bytes 163840

commit v3 on v1

--- a/solution.py
+++ b/solution.py
@@ -23,7 +23,9 @@
 
 
 def dot3(a_high, a_low, b_high, b_low):
-    return dot(a_high, b_high) + (dot(a_high, b_low) + dot(a_low, b_high))
+    rows = a_high.shape[0]
+    both = dot(jnp.concatenate([a_high, a_low], axis=0), b_high)
+    return both[:rows] + (both[rows:] + dot(a_high, b_low))
 
 
 def kernel(n_tens, n_atom, chibar, t_blocks, n_saved, q_list_in, q_count_in, out, q_list, q_count,
@@ -216,7 +218,7 @@
     inner = side(t) == 0
     edge = straddles(t)
 
-    for k in (0, 3, 1, 2):
+    for k in (3, 0, 1, 2):
         if k < 3:
             mbar[k][0].wait_recv()
         mbar[k][1].wait_recv()
@@ -246,6 +248,14 @@
                 def _():
                     part_home(i, o).start()
 
+    for k in range(STAGES):
+        for copy in chi[k]:
+            copy.wait_send()
+        forward[k].wait_send()
+        for e in range(2):
+            if (k, e) != (3, 0):
+                mbar[k][e].wait_send()
+
     order = (0, 1, 7, 2, 3, 4, 5)
 
     @pl.when(inner)
@@ -295,13 +305,6 @@
     out[:, 128:256] = jnp.where(half, lower[:, 128:], zero) + jnp.where(half, mid0, mid1) + upper[:, :128]
     out[:, 256:320] = upper[:, 128:192]
 
-    for k in range(STAGES):
-        for copy in chi[k]:
-            copy.wait_send()
-        forward[k].wait_send()
-        for e in range(2):
-            if (k, e) != (3, 0):
-                mbar[k][e].wait_send()
     for i in order:
         o = source(i // 2, i % 2)
         part(i, o).wait_send()

time: 63.7 us -> 62.6 us (0.983)
  Pallas kernels: 61.3 us -> 60.3 us
    pallas_call x1, Pallas kernels: 61.3 us -> 60.3 us  [local(): pl.pallas_call(body, out_shape=jax.ShapeDtypeStruct((64, 320), F32), in_s...]
where the time goes in v3:
time: 62.6 us; the launch traced here: 62.5 us
  Pallas kernels  60.3 us (96%)
  local copies, waits for them, and re-layouts  1.54 us (2%)
  between operations  0.66 us (1%)
    pallas_call x1, Pallas kernels, local(): pl.pallas_call(body, out_shape=jax.ShapeDtypeStruct((64, 320), F32), in_s...  60.3 us
    unnamed x1, local copies, waits for them, and re-layouts  1.54 us

profile of v3, /device:TPU:1, one launch (start us, length us, event | category | flops | bytes accessed | tf_op | source)
XLA Modules:
  0.0 62.5 jit_solution(17607325662458455097)
XLA Ops:
  0.7 60.3 %gradient.1 = f32[64,320]{1,0:T(8,128)} custom-call(f32[384,256]{1,0:T(8,128)} %refs_0_.1, f32[384,1536]{1,0:T(8,128)} %refs_1_.1, f32[48,12288]{1,0:T(8,128)} %refs_2_.1, s32[1,1,3]{2,1,0:T(1,128)} %refs_3_.1, s32[1,1]{1,0:T(1,128)S(6)} %copy.7.refs_4_), custom_call_target="tpu_custom_call" | custom-call | tf_op jit(solution)/shard_map/gradient/pallas_call | solution.py:330
  60.9 1.5 %copy.8 = f32[64,320]{1,0:T(8,128)} copy(f32[64,320]{1,0:T(8,128)} %gradient.1) | data formatting | bytes 163840

commit v4 on v3

--- a/solution.py
+++ b/solution.py
@@ -64,12 +64,12 @@
         copy.start()
     load_t = pltpu.make_async_copy(t_blocks, t_full, t_sem)
     load_n = pltpu.make_async_copy(n_saved, n_full, n_sem)
-    load_t.start()
     own = []
     for k in range(STAGES):
         rows = pl.ds(pl.multiple_of(target(k, 0) * 48, 48), 48)
         own.append(pltpu.make_async_copy(chibar.at[rows], near[k].at[REACH], own_sem.at[k]))
         own[k].start()
+    load_t.start()
     load_n.start()
 
     barrier = pltpu.get_barrier_semaphore()
@@ -84,7 +84,7 @@
         rows = pl.ds(pl.multiple_of(target(k, 0) * 48, 48), 48)
         chi.append([
             pltpu.make_async_remote_copy(
-                src_ref=chibar.at[rows],
+                src_ref=near[k].at[REACH],
                 dst_ref=near[k].at[REACH - by],
                 send_sem=chi_send.at[k, i],
                 recv_sem=chi_recv.at[k, i],
@@ -93,6 +93,8 @@
             )
             for i, by in enumerate(SHIFTS)
         ])
+    for copy in own:
+        copy.wait()
     for copy in chi[0]:
         copy.start()
 
@@ -180,7 +182,6 @@
     for copy in load_q:
         copy.wait()
     for k in range(STAGES):
-        own[k].wait()
         for copy in chi[k]:
             copy.wait_recv()
         forward[k].start()
@@ -291,6 +292,18 @@
     for i in (4, 3, 5, 2, 6, 1, 7):
         share(i).start()
     final[t] = total[...]
+    for i in order:
+        o = source(i // 2, i % 2)
+        part(i, o).wait_send()
+
+        @pl.when(straddles(o))
+        def _():
+            part_home(i, o).wait_send()
+
+    @pl.when(jnp.logical_not(inner))
+    def _():
+        part(6, t).wait_send()
+
     for i in range(1, n_tens):
         share(i).wait_recv()
 
@@ -304,18 +317,6 @@
     out[:, 0:128] = lower[:, :128] + jnp.where(half, zero, mid0)
     out[:, 128:256] = jnp.where(half, lower[:, 128:], zero) + jnp.where(half, mid0, mid1) + upper[:, :128]
     out[:, 256:320] = upper[:, 128:192]
-
-    for i in order:
-        o = source(i // 2, i % 2)
-        part(i, o).wait_send()
-
-        @pl.when(straddles(o))
-        def _():
-            part_home(i, o).wait_send()
-
-    @pl.when(jnp.logical_not(inner))
-    def _():
-        part(6, t).wait_send()
 
     for i in range(1, n_tens):
         share(i).wait_send()

time: 62.6 us -> 62.8 us (level)
  no operation moved by 1% of the time
where the time goes in v4:
time: 62.8 us; the launch traced here: 62.6 us
  Pallas kernels  60.4 us (96%)
  local copies, waits for them, and re-layouts  1.54 us (2%)
  between operations  0.66 us (1%)
    pallas_call x1, Pallas kernels, local(): pl.pallas_call(body, out_shape=jax.ShapeDtypeStruct((64, 320), F32), in_s...  60.4 us
    unnamed x1, local copies, waits for them, and re-layouts  1.54 us

profile of v4, /device:TPU:1, one launch (start us, length us, event | category | flops | bytes accessed | tf_op | source)
XLA Modules:
  0.0 62.6 jit_solution(6024198554370097356)
XLA Ops:
  0.7 60.4 %gradient.1 = f32[64,320]{1,0:T(8,128)} custom-call(f32[384,256]{1,0:T(8,128)} %refs_0_.1, f32[384,1536]{1,0:T(8,128)} %refs_1_.1, f32[48,12288]{1,0:T(8,128)} %refs_2_.1, s32[1,1,3]{2,1,0:T(1,128)} %refs_3_.1, s32[1,1]{1,0:T(1,128)S(6)} %copy.7.refs_4_), custom_call_target="tpu_custom_call" | custom-call | tf_op jit(solution)/shard_map/gradient/pallas_call | solution.py:331
  61.1 1.5 %copy.8 = f32[64,320]{1,0:T(8,128)} copy(f32[64,320]{1,0:T(8,128)} %gradient.1) | data formatting | bytes 163840
